TPU v7x, 32 devices: a whole 2x2x4 slice. The times are simulated.
32 devices in a mesh: pipe: 4 (over y, core), expert: 8 (over z, x).
Axes of the slice: x: 2, y: 2, z: 4, core: 2. Of those that a mesh axis runs over, the one named last changes fastest.
Arguments:
- fwd_tokens: bfloat16 [4, 64, 3584], P('pipe', 'expert'), may hold values from -6 to 6
- saved_tokens: bfloat16 [2, 4, 64, 3584], P(None, 'pipe', 'expert'), may hold values from -6 to 6
- cotangent: bfloat16 [4, 64, 3584], P('pipe', 'expert'), may hold values from -6 to 6
- fwd_routes: int32 [2, 4, 64, 2], P(None, 'pipe', 'expert'), may hold values from 0 to 3, all different within a row; in each aligned block of 8 rows (0 to 7, 8 to 15, ..., all dimensions but the last counted through in order) at most 5 rows name the same one
- bwd_routes: int32 [2, 4, 64, 2], P(None, 'pipe', 'expert'), may hold values from 0 to 3, all different within a row; in each aligned block of 8 rows (0 to 7, 8 to 15, ..., all dimensions but the last counted through in order) at most 5 rows name the same one
- norm_gain: float32 [4, 3584], P('pipe'), may hold values from 0.1 to 1.9
- router: bfloat16 [4, 3584, 4], P('pipe'), may hold values from -0.09375 to 0.09375
- w_gate: bfloat16 [4, 3584, 4096], P('pipe', None, 'expert'), may hold values from -0.09375 to 0.09375
- w_up: bfloat16 [4, 3584, 4096], P('pipe', None, 'expert'), may hold values from -0.09375 to 0.09375
- w_down: bfloat16 [4, 4096, 3584], P('pipe', 'expert'), may hold values from -0.1875 to 0.1875
Outputs:
- fwd_out: bfloat16 [4, 64, 3584], P('pipe', 'expert')
- bwd_out: bfloat16 [4, 64, 3584], P('pipe', 'expert')
Inputs may be any that keep to these rules, and one draw needn't show every extreme that they name: `fwd_routes`: each row names 2 different experts. In every aligned block of 8 rows (one device's tokens of one step and section) no expert is named more than 5 times; in at least one block some expert is named exactly 5 times. `bwd_routes`: each row names 2 different experts. In every aligned block of 8 rows (one device's tokens of one step and section) no expert is named more than 5 times; in at least one block some expert is named exactly 5 times.
All inputs are finite; a program needn't handle non-finite values.
Results may differ from a plain program's by a relative error of at most 0.018.
Values may be sent and summed in bfloat16 or wider, within the bound.
A program may use at most 64 MiB of HBM per device.

v0:
```python
import jax
import jax.numpy as jnp
from jax import lax
from jax.sharding import PartitionSpec as P


def from_behind(block, axis, distance):
    devices = range(lax.axis_size(axis))
    route = [((i - distance) % len(devices), i) for i in devices]
    return lax.ppermute(block, axis, route)


def norm_rows(values, norm_gain):
    wide = values.astype(jnp.float32)
    scale = lax.rsqrt(jnp.mean(wide * wide, axis=-1, keepdims=True) + 1e-06)
    return wide * scale * norm_gain


def gate_values(normed, router_w, routes, expert_count):
    logits = jnp.dot(normed, router_w, preferred_element_type=jnp.float32)
    sig_all = jax.nn.sigmoid(logits)
    route_pick = (routes[..., None] == jnp.arange(expert_count, dtype=jnp.int32)).astype(
        jnp.float32
    )
    chosen = jnp.sum(route_pick * sig_all[:, None, :], axis=-1)
    gate_total = jnp.sum(chosen, axis=-1, keepdims=True)
    gate_share = chosen / gate_total
    return (chosen, gate_total, gate_share, route_pick)


def slot_matrix(routes, expert_count, cap_rows):
    flat_routes = routes.reshape(-1)
    hit_table = (flat_routes[:, None] == jnp.arange(expert_count, dtype=jnp.int32)).astype(
        jnp.int32
    )
    before = jnp.cumsum(hit_table, axis=0) - hit_table
    slot_index = jnp.sum(before * hit_table, axis=1)
    position = flat_routes * cap_rows + slot_index
    placement = (position[:, None] == jnp.arange(expert_count * cap_rows, dtype=jnp.int32)).astype(
        jnp.float32
    )
    return placement.reshape(routes.shape[0], routes.shape[1], expert_count * cap_rows)


def expert_forward(row_block, gate_w, up_w, down_w):
    gate_pre = jnp.dot(row_block, gate_w, preferred_element_type=jnp.float32)
    up_pre = jnp.dot(row_block, up_w, preferred_element_type=jnp.float32)
    hidden = (jax.nn.silu(gate_pre) * up_pre).astype(jnp.bfloat16)
    return jnp.dot(hidden, down_w, preferred_element_type=jnp.float32).astype(jnp.bfloat16)


def expert_backward(row_block, cotan_rows, gate_w, up_w, down_w):
    gate_pre = jnp.dot(row_block, gate_w, preferred_element_type=jnp.float32)
    up_pre = jnp.dot(row_block, up_w, preferred_element_type=jnp.float32)
    gate_sig = jax.nn.sigmoid(gate_pre)
    gate_act = gate_pre * gate_sig
    hidden = (gate_act * up_pre).astype(jnp.bfloat16)
    expert_out = jnp.dot(hidden, down_w, preferred_element_type=jnp.float32).astype(jnp.bfloat16)
    hidden_grad = jnp.einsum("rd,fd->rf", cotan_rows, down_w, preferred_element_type=jnp.float32)
    gate_grad = (hidden_grad * up_pre * gate_sig * (1.0 + gate_pre * (1.0 - gate_sig))).astype(
        jnp.bfloat16
    )
    up_grad = (hidden_grad * gate_act).astype(jnp.bfloat16)
    row_grad = jnp.einsum("rf,df->rd", gate_grad, gate_w, preferred_element_type=jnp.float32)
    row_grad = row_grad + jnp.einsum("rf,df->rd", up_grad, up_w, preferred_element_type=jnp.float32)
    return (row_grad.astype(jnp.bfloat16), expert_out)


def token_grad(
    saved, cotan, norm_gain, router_w, chosen, gate_total, gate_share, route_pick, dgate, row_sum
):
    dchosen = (dgate - jnp.sum(gate_share * dgate, axis=-1, keepdims=True)) / gate_total
    logit_grad = dchosen * chosen * (1.0 - chosen)
    logit_full = jnp.einsum("tk,tke->te", logit_grad, route_pick, precision=lax.Precision.HIGHEST)
    router_back = jnp.dot(
        logit_full, router_w.astype(jnp.float32).T, precision=lax.Precision.HIGHEST
    )
    _, norm_pull = jax.vjp(lambda values: norm_rows(values, norm_gain), saved.astype(jnp.float32))
    return (cotan.astype(jnp.float32) + norm_pull(row_sum + router_back)[0]).astype(jnp.bfloat16)


def prepare_group(tokens_in, routes, norm_gain, router_w, expert_count, cap_rows):
    normed = norm_rows(tokens_in, norm_gain).astype(jnp.bfloat16)
    chosen, gate_total, gate_share, route_pick = gate_values(normed, router_w, routes, expert_count)
    gb_wide = gate_share.astype(jnp.bfloat16).astype(jnp.float32)
    placement = slot_matrix(routes, expert_count, cap_rows)
    spread = jnp.sum(placement, axis=1).astype(jnp.bfloat16)
    weighted = jnp.sum(placement * gb_wide[:, :, None], axis=1).astype(jnp.bfloat16)
    outgoing = jnp.einsum("tp,td->pd", spread, normed, preferred_element_type=jnp.float32).astype(
        jnp.bfloat16
    )
    outgoing = outgoing.reshape(expert_count, cap_rows, tokens_in.shape[-1])
    return (outgoing, (chosen, gate_total, gate_share, route_pick, placement, spread, weighted))


def local(
    fwd_tokens,
    saved_tokens,
    cotangent,
    fwd_routes,
    bwd_routes,
    norm_gain,
    router,
    w_gate,
    w_up,
    w_down,
):
    forward_in = fwd_tokens[0]
    cotan_in = cotangent[0]
    gain_row = norm_gain[0]
    router_w = router[0]
    gate_w = w_gate[0]
    up_w = w_up[0]
    down_w = w_down[0]
    tick_count = saved_tokens.shape[0]
    tok_rows = forward_in.shape[0]
    width = forward_in.shape[1]
    top_count = fwd_routes.shape[-1]
    expert_count = router_w.shape[1]
    cap_rows = 5 * tok_rows * top_count // (4 * expert_count)
    split_count = lax.axis_size("expert") // expert_count

    def fold_parts(received):
        return received.reshape(expert_count, split_count, cap_rows, width)

    for tick_index in range(tick_count):
        saved = saved_tokens[tick_index, 0]
        send_fwd, fwd_parts = prepare_group(
            forward_in, fwd_routes[tick_index, 0], gain_row, router_w, expert_count, cap_rows
        )
        send_saved, bwd_parts = prepare_group(
            saved, bwd_routes[tick_index, 0], gain_row, router_w, expert_count, cap_rows
        )
        chosen_b, total_b, share_b, pick_b, place_b, spread_b, weighted_b = bwd_parts
        send_cot = jnp.einsum(
            "tp,td->pd", weighted_b, cotan_in, preferred_element_type=jnp.float32
        ).astype(jnp.bfloat16)
        send_cot = send_cot.reshape(expert_count, cap_rows, width)
        send_fwd = jnp.repeat(send_fwd, split_count, axis=0)
        send_saved = jnp.repeat(send_saved, split_count, axis=0)
        send_cot = jnp.repeat(send_cot, split_count, axis=0)
        row_block = lax.all_to_all(send_fwd, "expert", split_axis=0, concat_axis=0, tiled=True)
        run_row_shape = row_block.shape
        result = expert_forward(row_block.reshape(-1, width), gate_w, up_w, down_w).reshape(
            run_row_shape
        )
        back_fwd = lax.all_to_all(result, "expert", split_axis=0, concat_axis=0, tiled=True)
        pieces = (
            lax.all_to_all(send_saved, "expert", split_axis=0, concat_axis=0, tiled=True),
            lax.all_to_all(send_cot, "expert", split_axis=0, concat_axis=0, tiled=True),
        )
        row_shape = pieces[0].shape
        grads, outs = expert_backward(
            pieces[0].reshape(-1, width), pieces[1].reshape(-1, width), gate_w, up_w, down_w
        )
        back_grad = lax.all_to_all(
            grads.reshape(row_shape), "expert", split_axis=0, concat_axis=0, tiled=True
        )
        back_out = lax.all_to_all(
            outs.reshape(row_shape), "expert", split_axis=0, concat_axis=0, tiled=True
        )
        weighted_f = fwd_parts[6].reshape(tok_rows, expert_count, cap_rows)
        mixture = jnp.einsum(
            "tec,ejcd->td", weighted_f, fold_parts(back_fwd), preferred_element_type=jnp.float32
        )
        fwd_result = (forward_in.astype(jnp.float32) + mixture).astype(jnp.bfloat16)
        spread_three = spread_b.reshape(tok_rows, expert_count, cap_rows)
        row_sum = jnp.einsum(
            "tec,ejcd->td", spread_three, fold_parts(back_grad), preferred_element_type=jnp.float32
        )
        place_four = place_b.astype(jnp.bfloat16).reshape(
            tok_rows, top_count, expert_count, cap_rows
        )
        out_route = jnp.einsum(
            "tkec,ejcd->tkd", place_four, fold_parts(back_out), preferred_element_type=jnp.float32
        )
        dgate = jnp.sum(out_route * cotan_in.astype(jnp.float32)[:, None, :], axis=-1)
        bwd_result = token_grad(
            saved, cotan_in, gain_row, router_w, chosen_b, total_b, share_b, pick_b, dgate, row_sum
        )
        if tick_index + 1 < tick_count:
            forward_in = from_behind(fwd_result, "pipe", 1)
            cotan_in = from_behind(bwd_result, "pipe", -1)
    return (fwd_result[None], bwd_result[None])


def solution(mesh):
    return jax.shard_map(
        local,
        mesh=mesh,
        in_specs=(
            P("pipe", "expert", None),
            P(None, "pipe", "expert", None),
            P("pipe", "expert", None),
            P(None, "pipe", "expert", None),
            P(None, "pipe", "expert", None),
            P("pipe", None),
            P("pipe", None, None),
            P("pipe", None, "expert"),
            P("pipe", None, "expert"),
            P("pipe", "expert", None),
        ),
        out_specs=(P("pipe", "expert", None), P("pipe", "expert", None)),
        check_vma=False,
    )
```

profile of v0, /device:TPU:0, one launch (start us, length us, event | category | flops | bytes accessed | tf_op | source)
XLA Modules:
  0.0 220.1 jit_solution(6537139482170593531)
XLA Ops:
  0.7 1.0 fusion.81
  3.6 0.8 reduce.6
  4.4 1.0 fusion.58
  6.3 1.1 convolution_convert_fusion.6
  7.4 0.8 broadcast_in_dim.24
  8.2 7.3 %all-to-all-start.5 = ((bf16[8,5,3584]{2,1,0:T(8,128)(2,1)}), bf16[8,5,3584]{2,1,0:T(8,128)(2,1)S(1)}, u32[]{:S(2)}, u32[]{:S(2)}) async-start(bf16[8,5,3584]{2,1,0:T(8,128)(2,1)} %bitcast.20), calls=%async_computation.5 | async-start | bytes 917504 | tf_op jit(solution)/shard_map/all_to_all | solution.py:149
  15.5 0.8 bitcast_convert_fusion
  16.3 1.1 convolution_convert_fusion.7
  17.3 1.0 fusion.93
  18.3 1.0 fusion.64
  19.4 0.7 fusion.193
  22.7 5.8 %all-to-all-done.5 = bf16[8,5,3584]{2,1,0:T(8,128)(2,1)S(1)} async-done(((bf16[8,5,3584]{2,1,0:T(8,128)(2,1)}), bf16[8,5,3584]{2,1,0:T(8,128)(2,1)S(1)}, u32[]{:S(2)}, u32[]{:S(2)}) %all-to-all-start.5) | async-done | bytes 286752 | tf_op jit(solution)/shard_map/all_to_all | solution.py:149
  28.5 0.8 broadcast_in_dim.23
  29.3 3.6 %all-to-all-start.4 = ((bf16[8,5,3584]{2,1,0:T(8,128)(2,1)}), bf16[8,5,3584]{2,1,0:T(8,128)(2,1)S(1)}, u32[]{:S(2)}, u32[]{:S(2)}) async-start(bf16[8,5,3584]{2,1,0:T(8,128)(2,1)} %bitcast.19), calls=%async_computation.4 | async-start | bytes 917504 | tf_op jit(solution)/shard_map/all_to_all | solution.py:150
  33.1 2.9 %fusion.34 = f32[40,512]{1,0:T(8,128)S(1)} fusion(bf16[40,3584]{1,0:T(8,128)(2,1)S(1)} %reshape.409, bf16[1,3584,512]{2,1,0:T(8,128)(2,1)} %param.17), kind=kOutput, calls=%fused_computation.54 | convolution fusion | flops 146800640 | bytes 4038656 | tf_op jit(solution)/shard_map/dot_general | solution.py:53
  36.2 0.7 fusion.22
  37.0 9.2 %all-to-all-done.4 = bf16[8,5,3584]{2,1,0:T(8,128)(2,1)S(1)} async-done(((bf16[8,5,3584]{2,1,0:T(8,128)(2,1)}), bf16[8,5,3584]{2,1,0:T(8,128)(2,1)S(1)}, u32[]{:S(2)}, u32[]{:S(2)}) %all-to-all-start.4) | async-done | bytes 286752 | tf_op jit(solution)/shard_map/all_to_all | solution.py:150
  46.1 0.8 broadcast_in_dim.20
  47.0 3.6 %all-to-all-start = ((bf16[8,5,3584]{2,1,0:T(8,128)(2,1)}), bf16[8,5,3584]{2,1,0:T(8,128)(2,1)S(1)}, u32[]{:S(2)}, u32[]{:S(2)}) async-start(bf16[8,5,3584]{2,1,0:T(8,128)(2,1)} %bitcast.4), calls=%async_computation | async-start | bytes 917504 | tf_op jit(solution)/shard_map/all_to_all | solution.py:142
  50.7 3.3 %fusion.14 = f32[40,512]{1,0:T(8,128)S(1)} fusion(bf16[40,3584]{1,0:T(8,128)(2,1)S(1)} %reshape.406, bf16[1,512,3584]{2,1,0:T(8,128)(2,1)} %param.19), kind=kOutput, calls=%fused_computation.34 | convolution fusion | flops 146800640 | bytes 4038656 | tf_op jit(solution)/shard_map/rd,fd->rf/dot_general | solution.py:59
  54.1 1.2 fusion.32
  55.3 0.7 convolution_convert_fusion.1
  56.0 0.9 reshape.411
  56.9 3.2 %fusion = bf16[40,3584]{1,0:T(8,128)(2,1)S(1)} fusion(f32[40,3584]{1,0:T(8,128)S(1)} %fusion.32, bf16[1,3584,512]{2,1,0:T(8,128)(2,1)} %param.18, f32[40,512]{1,0:T(8,128)S(1)} %fusion.14, f32[40,512]{1,0:T(8,128)S(1)} %fusion.34), kind=kOutput, calls=%fused_computation.2 | convolution fusion | flops 147210240 | bytes 4694016 | tf_op jit(solution)/shard_map/rf,df->rd/dot_general | solution.py:65
  60.2 3.7 %all-to-all-done = bf16[8,5,3584]{2,1,0:T(8,128)(2,1)S(1)} async-done(((bf16[8,5,3584]{2,1,0:T(8,128)(2,1)}), bf16[8,5,3584]{2,1,0:T(8,128)(2,1)S(1)}, u32[]{:S(2)}, u32[]{:S(2)}) %all-to-all-start) | async-done | bytes 286752 | tf_op jit(solution)/shard_map/all_to_all | solution.py:142
  63.9 3.6 %all-to-all-start.7 = ((bf16[8,5,3584]{2,1,0:T(8,128)(2,1)}), bf16[8,5,3584]{2,1,0:T(8,128)(2,1)S(1)}, u32[]{:S(2)}, u32[]{:S(2)}) async-start(bf16[8,5,3584]{2,1,0:T(8,128)(2,1)} %reshape.411), calls=%async_computation.7 | async-start | bytes 917504 | tf_op jit(solution)/shard_map/all_to_all | solution.py:159
  67.6 2.8 %fusion.38 = f32[40,512]{1,0:T(8,128)S(1)} fusion(bf16[40,3584]{1,0:T(8,128)(2,1)S(1)} %reshape.398, bf16[1,3584,512]{2,1,0:T(8,128)(2,1)} %param.17), kind=kOutput, calls=%fused_computation.58 | convolution fusion | flops 146800640 | bytes 4038656 | tf_op jit(solution)/shard_map/dot_general | solution.py:46
  70.4 0.9 reshape.410
  71.3 4.6 %convolution_convert_fusion.3 = bf16[40,3584]{1,0:T(8,128)(2,1)S(1)} fusion(bf16[1,512,3584]{2,1,0:T(8,128)(2,1)} %param.19, bf16[40,3584]{1,0:T(8,128)(2,1)S(1)} %reshape.398, bf16[1,3584,512]{2,1,0:T(8,128)(2,1)} %param.18, f32[40,512]{1,0:T(8,128)S(1)} %fusion.38), kind=kOutput, calls=%fused_computation.7 | convolution fusion | flops 293867520 | bytes 7995392 | tf_op jit(solution)/shard_map/dot_general | solution.py:49
  75.9 0.9 reshape.399
  76.8 3.9 %all-to-all-done.7 = bf16[8,5,3584]{2,1,0:T(8,128)(2,1)S(1)} async-done(((bf16[8,5,3584]{2,1,0:T(8,128)(2,1)}), bf16[8,5,3584]{2,1,0:T(8,128)(2,1)S(1)}, u32[]{:S(2)}, u32[]{:S(2)}) %all-to-all-start.7) | async-done | bytes 286752 | tf_op jit(solution)/shard_map/all_to_all | solution.py:159
  80.8 3.6 %all-to-all-start.6 = ((bf16[8,5,3584]{2,1,0:T(8,128)(2,1)}), bf16[8,5,3584]{2,1,0:T(8,128)(2,1)S(1)}, u32[]{:S(2)}, u32[]{:S(2)}) async-start(bf16[8,5,3584]{2,1,0:T(8,128)(2,1)} %reshape.410), calls=%async_computation.6 | async-start | bytes 917504 | tf_op jit(solution)/shard_map/all_to_all | solution.py:156
  85.0 12.7 %all-to-all-done.6 = bf16[8,5,3584]{2,1,0:T(8,128)(2,1)S(1)} async-done(((bf16[8,5,3584]{2,1,0:T(8,128)(2,1)}), bf16[8,5,3584]{2,1,0:T(8,128)(2,1)S(1)}, u32[]{:S(2)}, u32[]{:S(2)}) %all-to-all-start.6) | async-done | bytes 286752 | tf_op jit(solution)/shard_map/all_to_all | solution.py:156
  97.7 3.6 %all-to-all-start.1 = ((bf16[8,5,3584]{2,1,0:T(8,128)(2,1)}), bf16[8,5,3584]{2,1,0:T(8,128)(2,1)S(1)}, u32[]{:S(2)}, u32[]{:S(2)}) async-start(bf16[8,5,3584]{2,1,0:T(8,128)(2,1)} %reshape.399), calls=%async_computation.1 | async-start | bytes 917504 | tf_op jit(solution)/shard_map/all_to_all | solution.py:147
  103.0 0.9 collective-permute-start.1
  103.9 10.7 %all-to-all-done.1 = bf16[8,5,3584]{2,1,0:T(8,128)(2,1)S(1)} async-done(((bf16[8,5,3584]{2,1,0:T(8,128)(2,1)}), bf16[8,5,3584]{2,1,0:T(8,128)(2,1)S(1)}, u32[]{:S(2)}, u32[]{:S(2)}) %all-to-all-start.1) | async-done | bytes 286752 | tf_op jit(solution)/shard_map/all_to_all | solution.py:147
  114.6 0.8 broadcast_in_dim.27
  115.4 3.6 %all-to-all-start.9 = ((bf16[8,5,3584]{2,1,0:T(8,128)(2,1)}), bf16[8,5,3584]{2,1,0:T(8,128)(2,1)S(1)}, u32[]{:S(2)}, u32[]{:S(2)}) async-start(bf16[8,5,3584]{2,1,0:T(8,128)(2,1)} %bitcast.31), calls=%async_computation.9 | async-start | bytes 917504 | tf_op jit(solution)/shard_map/all_to_all | solution.py:149
  119.7 3.3 %collective-permute-done = bf16[8,3584]{1,0:T(8,128)(2,1)S(1)} collective-permute-done((bf16[8,3584]{1,0:T(8,128)(2,1)S(1)}, bf16[8,3584]{1,0:T(8,128)(2,1)S(1)}, u32[]{:S(2)}, u32[]{:S(2)}) %collective-permute-start) | collective-permute-done | bytes 57376 | tf_op jit(solution)/shard_map/ppermute | solution.py:10
  123.9 8.3 %all-to-all-done.9 = bf16[8,5,3584]{2,1,0:T(8,128)(2,1)S(1)} async-done(((bf16[8,5,3584]{2,1,0:T(8,128)(2,1)}), bf16[8,5,3584]{2,1,0:T(8,128)(2,1)S(1)}, u32[]{:S(2)}, u32[]{:S(2)}) %all-to-all-start.9) | async-done | bytes 286752 | tf_op jit(solution)/shard_map/all_to_all | solution.py:149
  132.3 0.8 broadcast_in_dim.26
  133.1 3.6 %all-to-all-start.8 = ((bf16[8,5,3584]{2,1,0:T(8,128)(2,1)}), bf16[8,5,3584]{2,1,0:T(8,128)(2,1)S(1)}, u32[]{:S(2)}, u32[]{:S(2)}) async-start(bf16[8,5,3584]{2,1,0:T(8,128)(2,1)} %bitcast.30), calls=%async_computation.8 | async-start | bytes 917504 | tf_op jit(solution)/shard_map/all_to_all | solution.py:150
  136.9 2.9 %fusion.19 = f32[40,512]{1,0:T(8,128)S(1)} fusion(bf16[40,3584]{1,0:T(8,128)(2,1)S(1)} %reshape.417, bf16[1,3584,512]{2,1,0:T(8,128)(2,1)} %param.18), kind=kOutput, calls=%fused_computation.39 | convolution fusion | flops 146800640 | bytes 4038656 | tf_op jit(solution)/shard_map/dot_general | solution.py:54
  140.0 0.7 fusion.30
  141.8 0.9 reshape.419
  142.7 7.2 %all-to-all-done.8 = bf16[8,5,3584]{2,1,0:T(8,128)(2,1)S(1)} async-done(((bf16[8,5,3584]{2,1,0:T(8,128)(2,1)}), bf16[8,5,3584]{2,1,0:T(8,128)(2,1)S(1)}, u32[]{:S(2)}, u32[]{:S(2)}) %all-to-all-start.8) | async-done | bytes 286752 | tf_op jit(solution)/shard_map/all_to_all | solution.py:150
  150.0 0.8 broadcast_in_dim.21
  150.8 3.7 %all-to-all-start.2 = ((bf16[8,5,3584]{2,1,0:T(8,128)(2,1)}), bf16[8,5,3584]{2,1,0:T(8,128)(2,1)S(1)}, u32[]{:S(2)}, u32[]{:S(2)}) async-start(bf16[8,5,3584]{2,1,0:T(8,128)(2,1)} %bitcast.11), calls=%async_computation.2 | async-start | bytes 917504 | tf_op jit(solution)/shard_map/all_to_all | solution.py:142
  154.6 3.3 %fusion.11 = f32[40,512]{1,0:T(8,128)S(1)} fusion(bf16[40,3584]{1,0:T(8,128)(2,1)S(1)} %reshape.414, bf16[1,512,3584]{2,1,0:T(8,128)(2,1)} %param.19), kind=kOutput, calls=%fused_computation.31 | convolution fusion | flops 146800640 | bytes 4038656 | tf_op jit(solution)/shard_map/rd,fd->rf/dot_general | solution.py:59
  158.0 1.2 fusion.28
  159.2 1.2 fusion.1
  160.4 7.3 %all-to-all-done.2 = bf16[8,5,3584]{2,1,0:T(8,128)(2,1)S(1)} async-done(((bf16[8,5,3584]{2,1,0:T(8,128)(2,1)}), bf16[8,5,3584]{2,1,0:T(8,128)(2,1)S(1)}, u32[]{:S(2)}, u32[]{:S(2)}) %all-to-all-start.2) | async-done | bytes 286752 | tf_op jit(solution)/shard_map/all_to_all | solution.py:142
  167.7 3.6 %all-to-all-start.11 = ((bf16[8,5,3584]{2,1,0:T(8,128)(2,1)}), bf16[8,5,3584]{2,1,0:T(8,128)(2,1)S(1)}, u32[]{:S(2)}, u32[]{:S(2)}) async-start(bf16[8,5,3584]{2,1,0:T(8,128)(2,1)} %reshape.419), calls=%async_computation.11 | async-start | bytes 917504 | tf_op jit(solution)/shard_map/all_to_all | solution.py:159
  171.5 2.8 %fusion.36 = f32[40,512]{1,0:T(8,128)S(1)} fusion(bf16[40,3584]{1,0:T(8,128)(2,1)S(1)} %reshape.402, bf16[1,3584,512]{2,1,0:T(8,128)(2,1)} %param.17), kind=kOutput, calls=%fused_computation.56 | convolution fusion | flops 146800640 | bytes 4038656 | tf_op jit(solution)/shard_map/dot_general | solution.py:46
  174.2 0.9 reshape.418
  175.1 4.6 %convolution_convert_fusion.2 = bf16[40,3584]{1,0:T(8,128)(2,1)S(1)} fusion(bf16[1,512,3584]{2,1,0:T(8,128)(2,1)} %param.19, bf16[40,3584]{1,0:T(8,128)(2,1)S(1)} %reshape.402, bf16[1,3584,512]{2,1,0:T(8,128)(2,1)} %param.18, f32[40,512]{1,0:T(8,128)S(1)} %fusion.36), kind=kOutput, calls=%fused_computation.6 | convolution fusion | flops 293867520 | bytes 7995392 | tf_op jit(solution)/shard_map/dot_general | solution.py:49
  179.7 0.9 reshape.403
  180.7 3.9 %all-to-all-done.11 = bf16[8,5,3584]{2,1,0:T(8,128)(2,1)S(1)} async-done(((bf16[8,5,3584]{2,1,0:T(8,128)(2,1)}), bf16[8,5,3584]{2,1,0:T(8,128)(2,1)S(1)}, u32[]{:S(2)}, u32[]{:S(2)}) %all-to-all-start.11) | async-done | bytes 286752 | tf_op jit(solution)/shard_map/all_to_all | solution.py:159
  184.6 3.6 %all-to-all-start.10 = ((bf16[8,5,3584]{2,1,0:T(8,128)(2,1)}), bf16[8,5,3584]{2,1,0:T(8,128)(2,1)S(1)}, u32[]{:S(2)}, u32[]{:S(2)}) async-start(bf16[8,5,3584]{2,1,0:T(8,128)(2,1)} %reshape.418), calls=%async_computation.10 | async-start | bytes 917504 | tf_op jit(solution)/shard_map/all_to_all | solution.py:156
  188.8 12.7 %all-to-all-done.10 = bf16[8,5,3584]{2,1,0:T(8,128)(2,1)S(1)} async-done(((bf16[8,5,3584]{2,1,0:T(8,128)(2,1)}), bf16[8,5,3584]{2,1,0:T(8,128)(2,1)S(1)}, u32[]{:S(2)}, u32[]{:S(2)}) %all-to-all-start.10) | async-done | bytes 286752 | tf_op jit(solution)/shard_map/all_to_all | solution.py:156
  201.5 3.6 %all-to-all-start.3 = ((bf16[8,5,3584]{2,1,0:T(8,128)(2,1)}), bf16[8,5,3584]{2,1,0:T(8,128)(2,1)S(1)}, u32[]{:S(2)}, u32[]{:S(2)}) async-start(bf16[8,5,3584]{2,1,0:T(8,128)(2,1)} %reshape.403), calls=%async_computation.3 | async-start | bytes 917504 | tf_op jit(solution)/shard_map/all_to_all | solution.py:147
  205.9 12.5 %all-to-all-done.3 = bf16[8,5,3584]{2,1,0:T(8,128)(2,1)S(1)} async-done(((bf16[8,5,3584]{2,1,0:T(8,128)(2,1)}), bf16[8,5,3584]{2,1,0:T(8,128)(2,1)S(1)}, u32[]{:S(2)}, u32[]{:S(2)}) %all-to-all-start.3) | async-done | bytes 286752 | tf_op jit(solution)/shard_map/all_to_all | solution.py:147
  218.5 0.7 fusion.117
  219.2 0.9 fusion.9
  (119 shorter events, 13.1 us)
Async XLA Ops:
  0.6 3.8 %copy-start = (bf16[1,3584,4]{1,2,0:T(4,128)(2,1)S(1)}, bf16[1,3584,4]{1,2,0:T(4,128)(2,1)}, u32[]{:S(2)}) copy-start(bf16[1,3584,4]{1,2,0:T(4,128)(2,1)} %param.16) | copy-start | bytes 86020
  0.6 21.7 %copy-start.10 = (bf16[1,8,3584]{2,1,0:T(8,128)(2,1)S(1)}, bf16[1,8,3584]{2,1,0:T(8,128)(2,1)}, u32[]{:S(2)}) copy-start(bf16[1,8,3584]{2,1,0:T(8,128)(2,1)} %param.10) | copy-start | bytes 172036
  8.2 20.3 %all-to-all-start.5 = ((bf16[8,5,3584]{2,1,0:T(8,128)(2,1)}), bf16[8,5,3584]{2,1,0:T(8,128)(2,1)S(1)}, u32[]{:S(2)}, u32[]{:S(2)}) async-start(bf16[8,5,3584]{2,1,0:T(8,128)(2,1)} %bitcast.20), calls=%async_computation.5 | async-start | bytes 917504 | tf_op jit(solution)/shard_map/all_to_all | solution.py:149
  29.3 16.8 %all-to-all-start.4 = ((bf16[8,5,3584]{2,1,0:T(8,128)(2,1)}), bf16[8,5,3584]{2,1,0:T(8,128)(2,1)S(1)}, u32[]{:S(2)}, u32[]{:S(2)}) async-start(bf16[8,5,3584]{2,1,0:T(8,128)(2,1)} %bitcast.19), calls=%async_computation.4 | async-start | bytes 917504 | tf_op jit(solution)/shard_map/all_to_all | solution.py:150
  33.1 3.1 %copy-start.6 = (bf16[1,3584,512]{2,1,0:T(8,128)(2,1)S(1)}, bf16[1,3584,512]{2,1,0:T(8,128)(2,1)}, u32[]{:S(2)}) copy-start(bf16[1,3584,512]{2,1,0:T(8,128)(2,1)} %param.18) | copy-start | bytes 11010052
  47.0 16.9 %all-to-all-start = ((bf16[8,5,3584]{2,1,0:T(8,128)(2,1)}), bf16[8,5,3584]{2,1,0:T(8,128)(2,1)S(1)}, u32[]{:S(2)}, u32[]{:S(2)}) async-start(bf16[8,5,3584]{2,1,0:T(8,128)(2,1)} %bitcast.4), calls=%async_computation | async-start | bytes 917504 | tf_op jit(solution)/shard_map/all_to_all | solution.py:142
  50.7 3.4 %copy-start.1 = (bf16[1,3584,512]{2,1,0:T(8,128)(2,1)S(1)}, bf16[1,3584,512]{2,1,0:T(8,128)(2,1)}, u32[]{:S(2)}) copy-start(bf16[1,3584,512]{2,1,0:T(8,128)(2,1)} %param.17) | copy-start | bytes 11010052
  50.7 4.6 %copy-start.4 = (bf16[1,512,3584]{2,1,0:T(8,128)(2,1)S(1)}, bf16[1,512,3584]{2,1,0:T(8,128)(2,1)}, u32[]{:S(2)}) copy-start(bf16[1,512,3584]{2,1,0:T(8,128)(2,1)} %param.19) | copy-start | bytes 11010052
  63.9 16.9 %all-to-all-start.7 = ((bf16[8,5,3584]{2,1,0:T(8,128)(2,1)}), bf16[8,5,3584]{2,1,0:T(8,128)(2,1)S(1)}, u32[]{:S(2)}, u32[]{:S(2)}) async-start(bf16[8,5,3584]{2,1,0:T(8,128)(2,1)} %reshape.411), calls=%async_computation.7 | async-start | bytes 917504 | tf_op jit(solution)/shard_map/all_to_all | solution.py:159
  75.9 25.8 %copy-start.8 = (bf16[2,1,8,3584]{3,2,1,0:T(8,128)(2,1)S(1)}, bf16[2,1,8,3584]{3,2,1,0:T(8,128)(2,1)}, u32[]{:S(2)}) copy-start(bf16[2,1,8,3584]{3,2,1,0:T(8,128)(2,1)} %param.11) | copy-start | bytes 344068
  75.9 26.9 %copy-start.9 = (bf16[1,8,3584]{2,1,0:T(8,128)(2,1)S(1)}, bf16[1,8,3584]{2,1,0:T(8,128)(2,1)}, u32[]{:S(2)}) copy-start(bf16[1,8,3584]{2,1,0:T(8,128)(2,1)} %param.12) | copy-start | bytes 172036
  80.8 16.9 %all-to-all-start.6 = ((bf16[8,5,3584]{2,1,0:T(8,128)(2,1)}), bf16[8,5,3584]{2,1,0:T(8,128)(2,1)S(1)}, u32[]{:S(2)}, u32[]{:S(2)}) async-start(bf16[8,5,3584]{2,1,0:T(8,128)(2,1)} %reshape.410), calls=%async_computation.6 | async-start | bytes 917504 | tf_op jit(solution)/shard_map/all_to_all | solution.py:156
  97.7 16.9 %all-to-all-start.1 = ((bf16[8,5,3584]{2,1,0:T(8,128)(2,1)}), bf16[8,5,3584]{2,1,0:T(8,128)(2,1)S(1)}, u32[]{:S(2)}, u32[]{:S(2)}) async-start(bf16[8,5,3584]{2,1,0:T(8,128)(2,1)} %reshape.399), calls=%async_computation.1 | async-start | bytes 917504 | tf_op jit(solution)/shard_map/all_to_all | solution.py:147
  103.0 16.4 %collective-permute-start.1 = (bf16[8,3584]{1,0:T(8,128)(2,1)S(1)}, bf16[8,3584]{1,0:T(8,128)(2,1)S(1)}, u32[]{:S(2)}, u32[]{:S(2)}) collective-permute-start(bf16[8,3584]{1,0:T(8,128)(2,1)S(1)} %fusion.102), channel_id=1, source_target_pairs={{8,0},{16,8},{24,16},{0,24},{9,1},{17,9},{25,17},{1,25},{10,2},{18... | collective-permute-start | bytes 172040 | tf_op jit(solution)/shard_map/ppermute | solution.py:10
  115.4 16.9 %all-to-all-start.9 = ((bf16[8,5,3584]{2,1,0:T(8,128)(2,1)}), bf16[8,5,3584]{2,1,0:T(8,128)(2,1)S(1)}, u32[]{:S(2)}, u32[]{:S(2)}) async-start(bf16[8,5,3584]{2,1,0:T(8,128)(2,1)} %bitcast.31), calls=%async_computation.9 | async-start | bytes 917504 | tf_op jit(solution)/shard_map/all_to_all | solution.py:149
  119.4 3.6 %collective-permute-start = (bf16[8,3584]{1,0:T(8,128)(2,1)S(1)}, bf16[8,3584]{1,0:T(8,128)(2,1)S(1)}, u32[]{:S(2)}, u32[]{:S(2)}) collective-permute-start(bf16[8,3584]{1,0:T(8,128)(2,1)S(1)} %fusion.8), channel_id=1, source_target_pairs={{24,0},{0,8},{8,16},{16,24},{25,1},{1,9},{9,17},{17,25},{26,2},{2,... | collective-permute-start | bytes 172040 | tf_op jit(solution)/shard_map/ppermute | solution.py:10
  133.1 16.9 %all-to-all-start.8 = ((bf16[8,5,3584]{2,1,0:T(8,128)(2,1)}), bf16[8,5,3584]{2,1,0:T(8,128)(2,1)S(1)}, u32[]{:S(2)}, u32[]{:S(2)}) async-start(bf16[8,5,3584]{2,1,0:T(8,128)(2,1)} %bitcast.30), calls=%async_computation.8 | async-start | bytes 917504 | tf_op jit(solution)/shard_map/all_to_all | solution.py:150
  136.8 3.1 %copy-start.2 = (bf16[1,3584,512]{2,1,0:T(8,128)(2,1)S(1)}, bf16[1,3584,512]{2,1,0:T(8,128)(2,1)}, u32[]{:S(2)}) copy-start(bf16[1,3584,512]{2,1,0:T(8,128)(2,1)} %param.17) | copy-start | bytes 11010052
  136.9 4.3 %copy-start.5 = (bf16[1,512,3584]{2,1,0:T(8,128)(2,1)S(1)}, bf16[1,512,3584]{2,1,0:T(8,128)(2,1)}, u32[]{:S(2)}) copy-start(bf16[1,512,3584]{2,1,0:T(8,128)(2,1)} %param.19) | copy-start | bytes 11010052
  150.8 16.9 %all-to-all-start.2 = ((bf16[8,5,3584]{2,1,0:T(8,128)(2,1)}), bf16[8,5,3584]{2,1,0:T(8,128)(2,1)S(1)}, u32[]{:S(2)}, u32[]{:S(2)}) async-start(bf16[8,5,3584]{2,1,0:T(8,128)(2,1)} %bitcast.11), calls=%async_computation.2 | async-start | bytes 917504 | tf_op jit(solution)/shard_map/all_to_all | solution.py:142
  154.6 3.4 %copy-start.3 = (bf16[1,3584,512]{2,1,0:T(8,128)(2,1)S(1)}, bf16[1,3584,512]{2,1,0:T(8,128)(2,1)}, u32[]{:S(2)}) copy-start(bf16[1,3584,512]{2,1,0:T(8,128)(2,1)} %param.17) | copy-start | bytes 11010052
  154.6 4.6 %copy-start.7 = (bf16[1,3584,512]{2,1,0:T(8,128)(2,1)S(1)}, bf16[1,3584,512]{2,1,0:T(8,128)(2,1)}, u32[]{:S(2)}) copy-start(bf16[1,3584,512]{2,1,0:T(8,128)(2,1)} %param.18) | copy-start | bytes 11010052
  167.7 16.9 %all-to-all-start.11 = ((bf16[8,5,3584]{2,1,0:T(8,128)(2,1)}), bf16[8,5,3584]{2,1,0:T(8,128)(2,1)S(1)}, u32[]{:S(2)}, u32[]{:S(2)}) async-start(bf16[8,5,3584]{2,1,0:T(8,128)(2,1)} %reshape.419), calls=%async_computation.11 | async-start | bytes 917504 | tf_op jit(solution)/shard_map/all_to_all | solution.py:159
  184.6 16.9 %all-to-all-start.10 = ((bf16[8,5,3584]{2,1,0:T(8,128)(2,1)}), bf16[8,5,3584]{2,1,0:T(8,128)(2,1)S(1)}, u32[]{:S(2)}, u32[]{:S(2)}) async-start(bf16[8,5,3584]{2,1,0:T(8,128)(2,1)} %reshape.418), calls=%async_computation.10 | async-start | bytes 917504 | tf_op jit(solution)/shard_map/all_to_all | solution.py:156
  201.5 16.9 %all-to-all-start.3 = ((bf16[8,5,3584]{2,1,0:T(8,128)(2,1)}), bf16[8,5,3584]{2,1,0:T(8,128)(2,1)S(1)}, u32[]{:S(2)}, u32[]{:S(2)}) async-start(bf16[8,5,3584]{2,1,0:T(8,128)(2,1)} %reshape.403), calls=%async_computation.3 | async-start | bytes 917504 | tf_op jit(solution)/shard_map/all_to_all | solution.py:147
where the time goes:
time: 222 us; the launch traced here: 220 us
  waiting for transfers between devices  101 us (45%)
  starting transfers between devices  48.2 us (22%)
  matrix products  45.9 us (21%)
  local copies, waits for them, and re-layouts  15.4 us (7%)
  other arithmetic  8.27 us (4%)
    all_to_all x2, waiting for transfers between devices, local(): lax.all_to_all(grads.reshape(row_shape), 'expert', split_axis=0, concat_a...  25.3 us
    all_to_all x2, waiting for transfers between devices, local(): lax.all_to_all(result, 'expert', split_axis=0, concat_axis=0, tiled=True)  23.1 us
    all_to_all x2, waiting for transfers between devices, local(): lax.all_to_all(send_cot, 'expert', split_axis=0, concat_axis=0, tiled=True)  16.4 us
    all_to_all x2, waiting for transfers between devices, local(): lax.all_to_all(send_saved, 'expert', split_axis=0, concat_axis=0, tiled=T...  14.1 us
    all_to_all x2, waiting for transfers between devices, local(): lax.all_to_all(send_fwd, 'expert', split_axis=0, concat_axis=0, tiled=True)  11 us
    all_to_all x2, starting transfers between devices, local(): lax.all_to_all(send_saved, 'expert', split_axis=0, concat_axis=0, tiled=T...  10.9 us
    dot_general x2, matrix products, expert_forward(): jnp.dot(hidden, down_w, preferred_element_type=jnp.float32)  9.2 us
    all_to_all x2, waiting for transfers between devices, local(): lax.all_to_all(outs.reshape(row_shape), 'expert', split_axis=0, concat_ax...  7.87 us
  transfers between devices with their start and end apart: 14, of which 13 were waited for; matrix products, arithmetic and copies ran while one was open for 26% of the time, Pallas kernels for 0%

commit v1 on v0

v1 whole, which is shorter than its diff:
```python
import jax
import jax.numpy as jnp
from jax import lax
from jax.sharding import PartitionSpec as P

F32 = jnp.float32
BF16 = jnp.bfloat16


def from_behind(block, axis, distance):
    devices = range(lax.axis_size(axis))
    route = [((i - distance) % len(devices), i) for i in devices]
    return lax.ppermute(block, axis, route)


def norm_rows(values, norm_gain):
    wide = values.astype(F32)
    scale = lax.rsqrt(jnp.mean(wide * wide, axis=-1, keepdims=True) + 1e-06)
    return wide * scale * norm_gain


def slots_of(hit):
    count = hit.shape[1]
    earlier = jnp.arange(count)[:, None] > jnp.arange(count)[None, :]
    return jnp.sum(jnp.where(earlier[None, :, :], hit[:, None, :], 0.0), axis=2)


def expert_place(hit, cap_rows):
    slot = slots_of(hit)
    lines = jnp.arange(cap_rows, dtype=F32)[None, :, None]
    return jnp.where((slot[:, None, :] == lines) & (hit[:, None, :] > 0), 1.0, 0.0)


def local(
    fwd_tokens,
    saved_tokens,
    cotangent,
    fwd_routes,
    bwd_routes,
    norm_gain,
    router,
    w_gate,
    w_up,
    w_down,
):
    x_in = fwd_tokens[0]
    c_in = cotangent[0]
    gain = norm_gain[0]
    router_w = router[0]
    gate_w, up_w, down_w = w_gate[0], w_up[0], w_down[0]
    ticks = saved_tokens.shape[0]
    tok, width = x_in.shape
    top = fwd_routes.shape[-1]
    experts = router_w.shape[1]
    cap = 5 * tok * top // (4 * experts)
    blocks = lax.axis_size("expert")
    split = blocks // experts
    mine = (lax.axis_index("expert") // split).astype(F32)
    rows = blocks * cap

    def gather(block):
        return lax.all_gather(block, "expert", axis=0, tiled=False)

    route_cols = jnp.concatenate(
        [fwd_routes[:, 0], bwd_routes[:, 0]], axis=0
    )
    route_cols = route_cols.transpose(1, 0, 2).reshape(tok, 2 * ticks * top).astype(BF16)
    route_cols = jnp.pad(route_cols, ((0, 0), (0, 128 - 2 * ticks * top)))
    wide_x = jnp.concatenate([x_in, route_cols], axis=1)
    zeros = jnp.zeros((2 * tok, 128), BF16)
    rest = jnp.concatenate([jnp.concatenate([saved_tokens[0, 0], c_in], axis=0), zeros], axis=1)
    first = gather(jnp.concatenate([wide_x, rest], axis=0))
    routes_all = (
        first[:, :tok, width : width + 2 * ticks * top]
        .astype(F32)
        .reshape(blocks, tok, 2 * ticks, top)
    )
    later = [None] + [gather(saved_tokens[t, 0]) for t in range(1, ticks)]

    def packed(values, routes):
        normed = norm_rows(values, gain).astype(BF16)
        logits = jnp.dot(
            normed.reshape(blocks * tok, width), router_w, preferred_element_type=F32
        ).reshape(blocks, tok, experts)
        sig = jax.nn.sigmoid(logits)
        pick = jnp.sum(
            (routes[..., None] == jnp.arange(experts, dtype=F32)).astype(F32), axis=2
        )
        total = jnp.sum(pick * sig, axis=-1)
        own = (jnp.arange(experts, dtype=F32) == mine).astype(F32)
        hit = jnp.sum(pick * own, axis=-1)
        share = jnp.sum(pick * sig * own, axis=-1) / total
        share = share.astype(BF16).astype(F32)
        place = expert_place(hit, cap)
        gate_rows = jnp.sum(place * share[:, None, :], axis=-1).reshape(rows, 1)
        place = place.astype(BF16)
        taken = jnp.einsum("npt,ntd->npd", place, normed, preferred_element_type=F32)
        return taken.astype(BF16).reshape(rows, width), gate_rows, place

    def owner_place(routes):
        pick = (routes[..., None] == jnp.arange(experts, dtype=jnp.int32)).astype(F32)
        hit = jnp.sum(pick, axis=1)
        slot = slots_of(hit.T)
        line = (slot.T[:, :, None] == jnp.arange(cap, dtype=F32)).astype(F32)
        spot = pick[:, :, :, None, None] * line[:, None, :, None, :]
        spot = jnp.broadcast_to(spot, (tok, top, experts, split, cap))
        return spot.reshape(tok, top, rows), pick

    for t in range(ticks):
        saved = saved_tokens[t, 0]
        if t == 0:
            x_all = first[:, :tok, :width]
            z_all = first[:, tok : 2 * tok, :width]
            c_all = first[:, 2 * tok :, :width]
        else:
            both = gather(jnp.concatenate([x_in, c_in], axis=0))
            x_all, c_all = both[:, :tok], both[:, tok:]
            z_all = later[t]
        m_rows, gate_b, place_b = packed(z_all, routes_all[:, :, ticks + t])
        c_rows = jnp.einsum("npt,ntd->npd", place_b, c_all, preferred_element_type=F32)
        c_rows = c_rows.astype(BF16).reshape(rows, width)
        u_rows, gate_f, _ = packed(x_all, routes_all[:, :, t])
        stacked = jnp.concatenate([u_rows, m_rows], axis=0)
        a = jnp.dot(stacked, gate_w, preferred_element_type=F32)
        b = jnp.dot(stacked, up_w, preferred_element_type=F32)
        sig_a = jax.nn.sigmoid(a)
        act = a * sig_a
        hidden = (act * b).astype(BF16)
        out = jnp.dot(hidden[:rows], down_w, preferred_element_type=F32) * gate_f
        raw_grad = jnp.einsum("rd,fd->rf", c_rows, down_w, preferred_element_type=F32)
        dgate_rows = jnp.sum(raw_grad * hidden[rows:].astype(F32), axis=1, keepdims=True)
        hidden_grad = raw_grad * gate_b
        a_b, b_b, sig_b, act_b = a[rows:], b[rows:], sig_a[rows:], act[rows:]
        gate_grad = (hidden_grad * b_b * sig_b * (1.0 + a_b * (1.0 - sig_b))).astype(BF16)
        up_grad = (hidden_grad * act_b).astype(BF16)
        row_grad = jnp.einsum("rf,df->rd", gate_grad, gate_w, preferred_element_type=F32)
        row_grad = row_grad + jnp.einsum("rf,df->rd", up_grad, up_w, preferred_element_type=F32)
        high = dgate_rows.astype(BF16)
        low = (dgate_rows - high.astype(F32)).astype(BF16)
        tail = jnp.pad(jnp.concatenate([high, low], axis=1), ((0, 0), (0, 126)))
        reply = jnp.concatenate([out.astype(BF16), row_grad.astype(BF16), tail], axis=1)
        span = reply.shape[1]
        reply = reply.reshape(blocks, cap * span // 128, 128)
        back = lax.all_to_all(reply, "expert", split_axis=0, concat_axis=0, tiled=True)
        back = back.reshape(rows, span)

        spot_f, _ = owner_place(fwd_routes[t, 0])
        spot_b, pick_b = owner_place(bwd_routes[t, 0])
        mixture = jnp.dot(
            jnp.sum(spot_f, axis=1).astype(BF16), back[:, :width], preferred_element_type=F32
        )
        row_sum = jnp.dot(
            jnp.sum(spot_b, axis=1).astype(BF16),
            back[:, width : 2 * width],
            preferred_element_type=F32,
        )
        dgate_got = jnp.sum(back[:, 2 * width : 2 * width + 2].astype(F32), axis=1)
        dgate = jnp.sum(spot_b * dgate_got, axis=-1)
        y = (x_in.astype(F32) + mixture).astype(BF16)

        normed_b = norm_rows(saved, gain).astype(BF16)
        sig_own = jax.nn.sigmoid(jnp.dot(normed_b, router_w, preferred_element_type=F32))
        chosen = jnp.sum(pick_b * sig_own[:, None, :], axis=-1)
        total = jnp.sum(chosen, axis=-1, keepdims=True)
        share = chosen / total
        dchosen = (dgate - jnp.sum(share * dgate, axis=-1, keepdims=True)) / total
        logit_grad = dchosen * chosen * (1.0 - chosen)
        logit_full = jnp.sum(logit_grad[..., None] * pick_b, axis=1)
        router_back = jnp.dot(
            logit_full, router_w.astype(F32).T, precision=lax.Precision.HIGHEST
        )
        _, norm_pull = jax.vjp(lambda values: norm_rows(values, gain), saved.astype(F32))
        dz = (c_in.astype(F32) + norm_pull(row_sum + router_back)[0]).astype(BF16)
        if t + 1 < ticks:
            x_in = from_behind(y, "pipe", 1)
            c_in = from_behind(dz, "pipe", -1)
    return (y[None], dz[None])


def solution(mesh):
    return jax.shard_map(
        local,
        mesh=mesh,
        in_specs=(
            P("pipe", "expert", None),
            P(None, "pipe", "expert", None),
            P("pipe", "expert", None),
            P(None, "pipe", "expert", None),
            P(None, "pipe", "expert", None),
            P("pipe", None),
            P("pipe", None, None),
            P("pipe", None, "expert"),
            P("pipe", None, "expert"),
            P("pipe", "expert", None),
        ),
        out_specs=(P("pipe", "expert", None), P("pipe", "expert", None)),
        check_vma=False,
    )
```

time: 222 us -> 187 us (0.84)
  blocking collectives: 0 us -> 66.6 us
  waiting for transfers between devices: 101 us -> 36 us
  starting transfers between devices: 48.2 us -> 8.66 us
  between operations: 1.09 us -> 14.6 us
  matrix products: 45.9 us -> 39.7 us
  local copies, waits for them, and re-layouts: 15.4 us -> 10.2 us
    all_to_all x12 -> x2, waiting for transfers between devices: 98 us -> 24.6 us  [local(): lax.all_to_all(reply, 'expert', split_axis=0, concat_axis=0, tiled=True)]
    all_gather x0 -> x2, blocking collectives: none -> 66.6 us  [gather(): return lax.all_gather(block, 'expert', axis=0, tiled=False)]
    all_to_all x12 -> x2, starting transfers between devices: 47.3 us -> 8.03 us  [local(): lax.all_to_all(reply, 'expert', split_axis=0, concat_axis=0, tiled=True)]
    all_gather x0 -> x1, waiting for transfers between devices: none -> 8.17 us  [gather(): return lax.all_gather(block, 'expert', axis=0, tiled=False)]
    dot_general x34 -> x30, matrix products: 45.9 us -> 39.7 us  [the longest x4 6.88 us: packed(): jnp.dot(normed.reshape(blocks * tok, width), router_w, preferred_element_...]
    broadcast_in_dim x6 -> x0, local copies, waits for them, and re-layouts: 4.84 us -> none  [the longest x2 1.63 us: local(): send_fwd = jnp.repeat(send_fwd, split_count, axis=0)]
    concatenate x0 -> x8, other arithmetic: none -> 2.46 us  [the longest x1 1.51 us: local(): first = gather(jnp.concatenate([wide_x, rest], axis=0))]
    reshape x18 -> x11, local copies, waits for them, and re-layouts: 6.61 us -> 5.29 us  [the longest x2 3.16 us: local(): reply = reply.reshape(blocks, cap * span // 128, 128)]
  transfers between devices with their start and end apart: 14 -> 5, of which waited for: 13 -> 5; matrix products, arithmetic and copies ran while one was open for 26% -> 5% of each run, Pallas kernels for 0% -> 0%
where the time goes in v1:
time: 187 us; the launch traced here: 186 us
  blocking collectives  66.6 us (36%)
  matrix products  39.7 us (21%)
  waiting for transfers between devices  36 us (19%)
  between operations  14.6 us (8%)
  local copies, waits for them, and re-layouts  10.2 us (5%)
  other arithmetic  9.82 us (5%)
  starting transfers between devices  8.66 us (5%)
    all_gather x2, blocking collectives, gather(): return lax.all_gather(block, 'expert', axis=0, tiled=False)  66.6 us
    all_to_all x2, waiting for transfers between devices, local(): lax.all_to_all(reply, 'expert', split_axis=0, concat_axis=0, tiled=True)  24.6 us
    all_gather x1, waiting for transfers between devices, gather(): return lax.all_gather(block, 'expert', axis=0, tiled=False)  8.17 us
    all_to_all x2, starting transfers between devices, local(): lax.all_to_all(reply, 'expert', split_axis=0, concat_axis=0, tiled=True)  8.03 us
    dot_general x4, matrix products, packed(): jnp.dot(normed.reshape(blocks * tok, width), router_w, preferred_element_...  6.88 us
    dot_general x2, matrix products, local(): jnp.einsum('rf,df->rd', gate_grad, gate_w, preferred_element_type=F32)  6.76 us
    dot_general x2, matrix products, local(): b = jnp.dot(stacked, up_w, preferred_element_type=F32)  5.87 us
    dot_general x2, matrix products, local(): out = jnp.dot(hidden[:rows], down_w, preferred_element_type=F32) * gate_f  5.54 us
  transfers between devices with their start and end apart: 5, of which 5 were waited for; matrix products, arithmetic and copies ran while one was open for 5% of the time, Pallas kernels for 0%

profile of v1, /device:TPU:0, one launch (start us, length us, event | category | flops | bytes accessed | tf_op | source)
XLA Modules:
  0.0 185.6 jit_solution(201380692073102680)
XLA Ops:
  7.2 0.7 convert_bitcast_fusion.1
  8.0 0.9 fusion.221
  8.9 0.8 fusion.92
  9.7 1.5 fusion.88
  11.2 1.0 fusion.93
  12.3 0.7 slice_bitcast_fusion.6
  13.0 0.7 slice_bitcast_fusion.8
  13.7 0.8 reduce.16
  14.5 1.0 fusion.50
  15.6 1.0 fusion.47
  17.0 33.9 %all-gather.2 = bf16[8,1,8,3584]{3,2,1,0:T(8,128)(2,1)S(1)} all-gather(bf16[1,1,8,3584]{3,2,1,0:T(8,128)(2,1)S(1)} %get-tuple-element.38), channel_id=4, replica_groups=mesh['pipe'=4,'expert'=8] {'expert'}, dimensions={0}, use_global_device_ids=true | all-gather | bytes 516096 | tf_op jit(solution)/shard_map/all_gather | solution.py:62
  50.9 0.2 fusion.60
  51.1 8.2 %all-gather.5.cloned.1.call-done = bf16[192,3712]{1,0:T(8,128)(2,1)} async-done(((bf16[24,3712]{1,0:T(8,128)(2,1)}), bf16[192,3712]{1,0:T(8,128)(2,1)}) %all-gather.5.cloned.1.call-update) | async-done | bytes 1425424 | tf_op jit(solution)/shard_map/all_gather | solution.py:62
  59.3 0.8 slice_convert_fusion
  60.1 1.4 fusion.54
  61.7 2.2 %fusion.40 = f32[8,8,4]{1,2,0:T(4,128)S(1)} fusion(f32[8,8]{1,0:T(8,128)S(1)} %add_rsqrt_fusion.2, f32[3584]{0:T(1024)S(1)} %reduce.16, bf16[8,24,3712]{2,1,0:T(8,128)(2,1)} %bitcast.177, bf16[1,3584,4]{1,2,0:T(4,128)(2,1)S(1)} %copy-done, f32[8,8,4]{1,0,2:T(8,128)S(1)} %convert_reduce_fusion.2), kind=kOutput, calls=%fused_computation.65 | convolution fusion | flops 2753536 | bytes 504064 | tf_op jit(solution)/shard_map/dot_general | solution.py:82
  64.0 2.2 %fusion.219 = (f32[8,8]{1,0:T(8,128)S(1)}, f32[8,8]{1,0:T(8,128)S(1)}, f32[8,8]{1,0:T(8,128)S(1)}, f32[8,8]{1,0:T(8,128)S(1)}, f32[8,8]{1,0:T(8,128)S(1)}, /*ind...) fusion(f32[4]{0:T(128)S(1)} %compare_convert_fusion, f32[8,8,4]{1,0,2:T(8,128)S(1)} %convert_reduce_fusion.3, ...), kind=kOutput, calls=%fused_computation.363 | convolution fusion | flops 2756608 | bytes 509200 | tf_op jit(solution)/shard_map/dot_general | solution.py:82
  66.4 0.3 convolution_convert_fusion.4
  66.7 0.3 convolution_convert_fusion.3
  67.0 0.1 reshape.461
  67.1 0.3 convolution_convert_fusion.5
  67.5 0.1 reshape.460
  67.6 0.1 reshape.462
  67.8 2.9 %fusion.17 = f32[80,512]{1,0:T(8,128)S(1)} fusion(bf16[80,3584]{1,0:T(8,128)(2,1)S(1)} %constant_dynamic-update-slice_fusion, bf16[1,3584,512]{2,1,0:T(8,128)(2,1)} %param.18), kind=kOutput, calls=%fused_computation.30 | convolution fusion | flops 293601280 | bytes 4407296 | tf_op jit(solution)/shard_map/dot_general | solution.py:125
  70.7 0.2 copy-done.1
  70.9 0.8 fusion.215
  71.7 0.3 copy-done.3
  72.0 1.3 multiply_reduce_fusion.1
  73.5 2.8 %fusion = bf16[40,3584]{1,0:T(8,128)(2,1)S(1)} fusion(bf16[1,512,3584]{2,1,0:T(8,128)(2,1)} %param.19, f32[40]{0:T(128)S(1)} %mul.576, bf16[80,512]{1,0:T(8,128)(2,1)S(1)} %get-tuple-element.36), kind=kOutput, calls=%fused_computation.10 | convolution fusion | flops 147087360 | bytes 3998208 | tf_op jit(solution)/shard_map/dot_general | solution.py:129
  76.6 3.4 %fusion.23 = f32[40,3584]{1,0:T(8,128)S(1)} fusion(bf16[1,3584,512]{2,1,0:T(8,128)(2,1)} %param.17, f32[80,512]{1,0:T(8,128)S(1)} %get-tuple-element.56, f32[80,512]{1,0:T(8,128)S(1)} %fusion.17, f32[80,512]{1,0:T(8,128)S(1)} %get-tuple-element.37, f32[40,512]{1,0:T(8,128)S(1)} %get-tuple-element.58, f32[40]{0:T(128)S(1)} %mul.583), kind=kOutput, calls=%fused_computation.36 | convolution fusion | flops 146964480 | bytes 4571648 | tf_op jit(solution)/shard_map/rf,df->rd/dot_general | solution.py:136
  80.0 1.2 fusion.1
  81.3 1.6 reshape.463
  82.9 3.6 %all-to-all-start = ((bf16[8,285,128]{2,1,0:T(8,128)(2,1)}), bf16[8,285,128]{2,1,0:T(8,128)(2,1)S(1)}, u32[]{:S(2)}, u32[]{:S(2)}) async-start(bf16[8,285,128]{2,1,0:T(8,128)(2,1)} %reshape.463), calls=%async_computation | async-start | bytes 1179648 | tf_op jit(solution)/shard_map/all_to_all | solution.py:144
  86.7 1.2 fusion.32
  87.9 0.3 convolution_convert_fusion.1
  88.3 14.2 %all-to-all-done = bf16[8,285,128]{2,1,0:T(8,128)(2,1)S(1)} async-done(((bf16[8,285,128]{2,1,0:T(8,128)(2,1)}), bf16[8,285,128]{2,1,0:T(8,128)(2,1)S(1)}, u32[]{:S(2)}, u32[]{:S(2)}) %all-to-all-start) | async-done | bytes 583712 | tf_op jit(solution)/shard_map/all_to_all | solution.py:144
  102.4 0.6 reshape.464
  103.5 0.2 fusion.76
  103.7 0.4 fusion.98
  104.3 0.2 fusion.6
  104.5 0.5 collective-permute-start
  105.2 1.0 collective-permute-done.1
  106.1 2.2 %collective-permute-done = bf16[8,3584]{1,0:T(8,128)(2,1)S(1)} collective-permute-done((bf16[8,3584]{1,0:T(8,128)(2,1)S(1)}, bf16[8,3584]{1,0:T(8,128)(2,1)S(1)}, u32[]{:S(2)}, u32[]{:S(2)}) %collective-permute-start) | collective-permute-done | bytes 57376 | tf_op jit(solution)/shard_map/ppermute | solution.py:13
  108.3 32.7 %all-gather.1 = bf16[128,3584]{1,0:T(8,128)(2,1)S(1)} all-gather(bf16[16,3584]{1,0:T(8,128)(2,1)S(1)} %pad_maximum_fusion), channel_id=3, replica_groups=mesh['pipe'=4,'expert'=8] {'expert'}, dimensions={0}, use_global_device_ids=true | all-gather | bytes 1032192 | tf_op jit(solution)/shard_map/all_gather | solution.py:62
  141.0 0.2 fusion.57
  141.2 0.3 convolution_convert_fusion
  141.5 0.3 convolution_convert_fusion.2
  141.9 0.1 reshape.465
  142.1 2.9 %fusion.14 = f32[80,512]{1,0:T(8,128)S(1)} fusion(bf16[80,3584]{1,0:T(8,128)(2,1)S(1)} %constant_dynamic-update-slice_fusion.2, bf16[1,3584,512]{2,1,0:T(8,128)(2,1)} %param.18), kind=kOutput, calls=%fused_computation.27 | convolution fusion | flops 293601280 | bytes 4407296 | tf_op jit(solution)/shard_map/dot_general | solution.py:125
  145.0 0.1 copy-done.2
  145.1 0.8 fusion.216
  146.1 3.3 %multiply_reduce_fusion = (f32[40]{0:T(128)S(1)}, f32[40,512]{1,0:T(8,128)S(1)}) fusion(bf16[80,512]{1,0:T(8,128)(2,1)S(1)} %get-tuple-element.33, bf16[40,3584]{1,0:T(8,128)(2,1)S(1)} %reshape.467, bf16[1,512,3584]{2,1,0:T(8,128)(2,1)} %param.19), kind=kOutput, calls=%fused_computation.156 | convolution fusion | flops 146862048 | bytes 4079776 | tf_op jit(solution)/shard_map/rd,fd->rf/dot_general | solution.py:130
  149.4 1.2 fusion.217
  150.8 2.8 %fusion.2 = bf16[40,3584]{1,0:T(8,128)(2,1)S(1)} fusion(bf16[1,512,3584]{2,1,0:T(8,128)(2,1)} %param.19, f32[40]{0:T(128)S(1)} %mul.640, bf16[80,512]{1,0:T(8,128)(2,1)S(1)} %get-tuple-element.33), kind=kOutput, calls=%fused_computation.12 | convolution fusion | flops 147087360 | bytes 3998208 | tf_op jit(solution)/shard_map/dot_general | solution.py:129
  153.9 3.4 %fusion.19 = f32[40,3584]{1,0:T(8,128)S(1)} fusion(bf16[1,3584,512]{2,1,0:T(8,128)(2,1)} %param.17, f32[80,512]{1,0:T(8,128)S(1)} %get-tuple-element.61, f32[80,512]{1,0:T(8,128)S(1)} %fusion.14, f32[80,512]{1,0:T(8,128)S(1)} %get-tuple-element.34, f32[40,512]{1,0:T(8,128)S(1)} %get-tuple-element.63, f32[40]{0:T(128)S(1)} %mul.647), kind=kOutput, calls=%fused_computation.32 | convolution fusion | flops 146964480 | bytes 4571648 | tf_op jit(solution)/shard_map/rf,df->rd/dot_general | solution.py:136
  157.3 1.2 fusion.3
  158.6 1.6 reshape.468
  160.1 4.5 %all-to-all-start.1 = ((bf16[8,285,128]{2,1,0:T(8,128)(2,1)}), bf16[8,285,128]{2,1,0:T(8,128)(2,1)S(1)}, u32[]{:S(2)}, u32[]{:S(2)}) async-start(bf16[8,285,128]{2,1,0:T(8,128)(2,1)} %reshape.468), calls=%async_computation.1 | async-start | bytes 1179648 | tf_op jit(solution)/shard_map/all_to_all | solution.py:144
  165.1 10.5 %all-to-all-done.1 = bf16[8,285,128]{2,1,0:T(8,128)(2,1)S(1)} async-done(((bf16[8,285,128]{2,1,0:T(8,128)(2,1)}), bf16[8,285,128]{2,1,0:T(8,128)(2,1)S(1)}, u32[]{:S(2)}, u32[]{:S(2)}) %all-to-all-start.1) | async-done | bytes 583712 | tf_op jit(solution)/shard_map/all_to_all | solution.py:144
  175.6 0.6 reshape.469
  176.7 0.2 fusion.72
  176.9 0.4 fusion.94
  177.3 0.8 fusion.115
  178.1 0.7 fusion.116
  (114 shorter events, 4.2 us)
Async XLA Ops:
  7.2 7.3 %copy-start = (bf16[1,3584,4]{1,2,0:T(4,128)(2,1)S(1)}, bf16[1,3584,4]{1,2,0:T(4,128)(2,1)}, u32[]{:S(2)}) copy-start(bf16[1,3584,4]{1,2,0:T(4,128)(2,1)} %param.16) | copy-start | bytes 86020
  7.2 52.1 %all-gather.5.cloned.1.call-start = ((), (), s32[]{:S(2)}) async-start(), calls=%async_computation.2 | async-start | bytes 1603584 | tf_op jit(solution)/shard_map/all_gather | solution.py:62
  59.3 7.0 %copy-start.7 = (bf16[192,3712]{1,0:T(8,128)(2,1)S(1)}, bf16[192,3712]{1,0:T(8,128)(2,1)}, u32[]{:S(2)}) copy-start(bf16[192,3712]{1,0:T(8,128)(2,1)} %all-gather.5.cloned.1.call-done) | copy-start | bytes 4276228
  67.7 3.1 %copy-start.1 = (bf16[1,3584,512]{2,1,0:T(8,128)(2,1)S(1)}, bf16[1,3584,512]{2,1,0:T(8,128)(2,1)}, u32[]{:S(2)}) copy-start(bf16[1,3584,512]{2,1,0:T(8,128)(2,1)} %param.17) | copy-start | bytes 11010052
  67.8 4.2 %copy-start.3 = (bf16[1,512,3584]{2,1,0:T(8,128)(2,1)S(1)}, bf16[1,512,3584]{2,1,0:T(8,128)(2,1)}, u32[]{:S(2)}) copy-start(bf16[1,512,3584]{2,1,0:T(8,128)(2,1)} %param.19) | copy-start | bytes 11010052
  76.6 3.4 %copy-start.4 = (bf16[1,3584,512]{2,1,0:T(8,128)(2,1)S(1)}, bf16[1,3584,512]{2,1,0:T(8,128)(2,1)}, u32[]{:S(2)}) copy-start(bf16[1,3584,512]{2,1,0:T(8,128)(2,1)} %param.18) | copy-start | bytes 11010052
  81.2 22.5 %copy-start.6 = (bf16[2,1,8,3584]{3,2,1,0:T(8,128)(2,1)S(1)}, bf16[2,1,8,3584]{3,2,1,0:T(8,128)(2,1)}, u32[]{:S(2)}) copy-start(bf16[2,1,8,3584]{3,2,1,0:T(8,128)(2,1)} %param.11) | copy-start | bytes 344068
  81.2 22.9 %copy-start.8 = (bf16[1,8,3584]{2,1,0:T(8,128)(2,1)S(1)}, bf16[1,8,3584]{2,1,0:T(8,128)(2,1)}, u32[]{:S(2)}) copy-start(bf16[1,8,3584]{2,1,0:T(8,128)(2,1)} %param.12) | copy-start | bytes 172036
  81.2 23.1 %copy-start.9 = (bf16[1,8,3584]{2,1,0:T(8,128)(2,1)S(1)}, bf16[1,8,3584]{2,1,0:T(8,128)(2,1)}, u32[]{:S(2)}) copy-start(bf16[1,8,3584]{2,1,0:T(8,128)(2,1)} %param.10) | copy-start | bytes 172036
  82.9 19.6 %all-to-all-start = ((bf16[8,285,128]{2,1,0:T(8,128)(2,1)}), bf16[8,285,128]{2,1,0:T(8,128)(2,1)S(1)}, u32[]{:S(2)}, u32[]{:S(2)}) async-start(bf16[8,285,128]{2,1,0:T(8,128)(2,1)} %reshape.463), calls=%async_computation | async-start | bytes 1179648 | tf_op jit(solution)/shard_map/all_to_all | solution.py:144
  104.2 1.9 %collective-permute-start.1 = (bf16[8,3584]{1,0:T(8,128)(2,1)S(1)}, bf16[8,3584]{1,0:T(8,128)(2,1)S(1)}, u32[]{:S(2)}, u32[]{:S(2)}) collective-permute-start(bf16[8,3584]{1,0:T(8,128)(2,1)S(1)} %fusion.100), channel_id=1, source_target_pairs={{8,0},{16,8},{24,16},{0,24},{9,1},{17,9},{25,17},{1,25},{10,2},{18... | collective-permute-start | bytes 172040 | tf_op jit(solution)/shard_map/ppermute | solution.py:13
  104.5 3.8 %collective-permute-start = (bf16[8,3584]{1,0:T(8,128)(2,1)S(1)}, bf16[8,3584]{1,0:T(8,128)(2,1)S(1)}, u32[]{:S(2)}, u32[]{:S(2)}) collective-permute-start(bf16[8,3584]{1,0:T(8,128)(2,1)S(1)} %fusion.6), channel_id=1, source_target_pairs={{24,0},{0,8},{8,16},{16,24},{25,1},{1,9},{9,17},{17,25},{26,2},{2,... | collective-permute-start | bytes 172040 | tf_op jit(solution)/shard_map/ppermute | solution.py:13
  142.0 3.1 %copy-start.2 = (bf16[1,3584,512]{2,1,0:T(8,128)(2,1)S(1)}, bf16[1,3584,512]{2,1,0:T(8,128)(2,1)}, u32[]{:S(2)}) copy-start(bf16[1,3584,512]{2,1,0:T(8,128)(2,1)} %param.17) | copy-start | bytes 11010052
  153.9 3.4 %copy-start.5 = (bf16[1,3584,512]{2,1,0:T(8,128)(2,1)S(1)}, bf16[1,3584,512]{2,1,0:T(8,128)(2,1)}, u32[]{:S(2)}) copy-start(bf16[1,3584,512]{2,1,0:T(8,128)(2,1)} %param.18) | copy-start | bytes 11010052
  160.1 15.4 %all-to-all-start.1 = ((bf16[8,285,128]{2,1,0:T(8,128)(2,1)}), bf16[8,285,128]{2,1,0:T(8,128)(2,1)S(1)}, u32[]{:S(2)}, u32[]{:S(2)}) async-start(bf16[8,285,128]{2,1,0:T(8,128)(2,1)} %reshape.468), calls=%async_computation.1 | async-start | bytes 1179648 | tf_op jit(solution)/shard_map/all_to_all | solution.py:144
Sparse Core Ops, SparseCore 0:
  11.4 47.8 all-gather.4
